TPU v7x, 32 devices: a whole 2x2x4 slice. The times are simulated.
32 devices in a mesh: blk: 4 (over x, core), grp: 8 (over z, y).
Axes of the slice: x: 2, y: 2, z: 4, core: 2. Of those that a mesh axis runs over, the one named last changes fastest.
Arguments:
- picture_integer_codes: bfloat16 [896, 768], P(('blk', 'grp')), may hold values from -4 to 4
- picture_code_multiplier: float32 [896], P(('blk', 'grp')), may hold values from 0.01 to 0.1
- caption_integer_codes: bfloat16 [896, 768], P(('blk', 'grp')), may hold values from -4 to 4
- caption_code_multiplier: float32 [896], P(('blk', 'grp')), may hold values from 0.01 to 0.1
- sharpness_factor: float32 [1], replicated, may hold values from 5 to 15
- similarity_shift: float32 [1], replicated, may hold values from -6 to -2
Outputs:
- loss: float32 [1], replicated
- image_grad: float32 [896, 768], P(('blk', 'grp'))
- text_grad: float32 [896, 768], P(('blk', 'grp'))
- temp_grad: float32 [1], replicated
- bias_grad: float32 [1], replicated
All inputs are finite; a program needn't handle non-finite values.
Results may differ from a plain program's by a relative error of at most 0.0041.
Values may be sent and summed in bfloat16 or wider, within the bound.
A program may use at most 64 MiB of HBM per device.

v0:
```python
import jax
import jax.numpy as jnp
from jax import lax
from jax.sharding import PartitionSpec as P


def score_block(wide, piece, row_base, column_offset, shard_rows, sharpness_number, bias_value):
    dots = lax.dot_general(
        piece, wide, (((1,), (1,)), ((), ())), preferred_element_type=jnp.float32
    )
    logits = sharpness_number * dots + bias_value
    local = jnp.arange(piece.shape[0], dtype=jnp.int32) - row_base
    cross_total = jnp.arange(wide.shape[0], dtype=jnp.int32) - column_offset
    inside = (local >= 0) & (local < shard_rows)
    positive = (local[:, None] == cross_total[None, :]) & inside[:, None]
    slopes = jax.nn.sigmoid(logits) - positive.astype(jnp.float32)
    loss_terms = jnp.where(positive, jax.nn.softplus(-logits), jax.nn.softplus(logits))
    weights = (sharpness_number * slopes).astype(jnp.bfloat16)
    piece_grad = jnp.dot(weights, wide, preferred_element_type=jnp.float32)
    wide_part = lax.dot_general(
        weights, piece, (((0,), (0,)), ((), ())), preferred_element_type=jnp.float32
    )
    sums = jnp.stack([jnp.sum(loss_terms), jnp.sum(slopes * dots), jnp.sum(slopes)])
    return (piece_grad, wide_part, sums)


def body(
    picture_integer_codes,
    picture_code_multiplier,
    caption_integer_codes,
    caption_code_multiplier,
    sharpness_factor,
    similarity_shift,
):
    images = (picture_code_multiplier[:, None] * picture_integer_codes.astype(jnp.float32)).astype(
        jnp.bfloat16
    )
    texts = (caption_code_multiplier[:, None] * caption_integer_codes.astype(jnp.float32)).astype(
        jnp.bfloat16
    )
    shard_rows = images.shape[0]
    groups = lax.axis_size("blk")
    members = lax.axis_size("grp")
    row_base = lax.axis_index("blk") * shard_rows
    column_offset = lax.axis_index("grp") * shard_rows
    sharpness_number = sharpness_factor[0]
    bias_value = similarity_shift[0]
    wide_source, narrow_source = (images, texts)
    wide = lax.all_gather(wide_source, "grp", axis=0, tiled=True)
    narrow = lax.all_gather(narrow_source, "blk", axis=0, tiled=True)
    narrow_total, wide_total, sums = score_block(
        wide, narrow, row_base, column_offset, shard_rows, sharpness_number, bias_value
    )
    wide_grad = lax.psum_scatter(wide_total, "grp", scatter_dimension=0, tiled=True)
    narrow_grad = lax.psum_scatter(narrow_total, "blk", scatter_dimension=0, tiled=True)
    totals = lax.psum(sums, ("blk", "grp"))
    totals = totals / (shard_rows * groups * members)
    image_grad, text_grad = (wide_grad, narrow_grad)
    return (totals[0:1], image_grad, text_grad, totals[1:2], totals[2:3])


def solution(mesh):
    placed = (
        P(("blk", "grp"), None),
        P(("blk", "grp")),
        P(("blk", "grp"), None),
        P(("blk", "grp")),
        P(),
        P(),
    )
    return jax.shard_map(
        body,
        mesh=mesh,
        in_specs=placed,
        out_specs=(P(), P(("blk", "grp"), None), P(("blk", "grp"), None), P(), P()),
        check_vma=False,
    )
```

profile of v0, /device:TPU:0, one launch (start us, length us, event | category | flops | bytes accessed | tf_op | source)
XLA Modules:
  0.0 129.3 jit_solution(14750957754643576356)
XLA Ops:
  2.0 0.0 copy-start.1
  2.0 0.6 copy-done.1
  2.6 0.9 fusion.4
  3.5 6.8 %all-gather = bf16[4,28,768]{2,1,0:T(8,128)(2,1)S(1)} all-gather(bf16[1,28,768]{2,1,0:T(8,128)(2,1)S(1)} %fusion.4), channel_id=1, replica_groups=mesh['blk'=4,'grp'=8] {'blk'}, dimensions={0}, use_global_device_ids=true | all-gather | bytes 215040 | tf_op jit(solution)/shard_map/all_gather | solution.py:50
  10.3 0.0 copy-start
  10.3 0.0 copy-start.2
  10.4 0.8 copy-done
  11.1 0.0 copy-done.2
  11.1 0.1 fusion.5
  11.2 31.7 %all-gather.1 = bf16[8,28,768]{2,1,0:T(8,128)(2,1)S(1)} all-gather(bf16[1,28,768]{2,1,0:T(8,128)(2,1)S(1)} %fusion.5), channel_id=1, replica_groups=mesh['blk'=4,'grp'=8] {'grp'}, dimensions={0}, use_global_device_ids=true | all-gather | bytes 387072 | tf_op jit(solution)/shard_map/all_gather | solution.py:49
  42.9 0.1 reshape.28
  43.0 1.1 fusion.3
  44.1 0.2 fusion.6
  44.3 9.8 %fusion.1 = f32[32,768]{1,0:T(8,128)S(1)} fusion(f32[112,768]{1,0:T(8,128)S(1)} %fusion.6), kind=kCustom, calls=%all-reduce-scatter.1 | all-reduce-scatter fusion | flops 98305 | bytes 442880
  54.1 1.3 collective-permute-start.1
  55.4 0.4 fusion.7
  55.8 26.2 %fusion = f32[32,768]{1,0:T(8,128)S(1)} fusion(f32[224,768]{1,0:T(8,128)S(1)} %fusion.7), kind=kCustom, calls=%all-reduce-scatter | all-reduce-scatter fusion | flops 196609 | bytes 786944
  82.0 2.0 %pad_maximum_fusion = f32[3]{0:T(128)S(1)} fusion(f32[1]{0:T(128)} %bitcast.6, f32[1]{0:T(128)} %bitcast.5, f32[1]{0:T(128)} %bitcast.4), kind=kLoop, calls=%fused_computation.20 | loop fusion | flops 6 | bytes 24 | tf_op jit(solution)/shard_map/stack | solution.py:23
  84.0 1.7 %collective-permute-start = (f32[28,768]{1,0:T(8,128)S(1)}, f32[28,768]{1,0:T(8,128)S(1)}, u32[]{:S(2)}, u32[]{:S(2)}) collective-permute-start(f32[28,768]{1,0:T(8,128)S(1)} %slice.12), channel_id=1, source_target_pairs={{0,1},{1,2},{2,3},{3,4},{4,5},{5,6},{6,7},{8,9},{9,10},{10,11},{11... | collective-permute-start | bytes 258056
  85.7 38.1 %psum.7 = f32[3]{0:T(128)S(1)} all-reduce(f32[3]{0:T(128)S(1)} %pad_maximum_fusion), channel_id=1, replica_groups=mesh['blk'=4,'grp'=8] {'blk','grp'}, use_global_device_ids=true, to_apply=%region_3.4 | all-reduce | flops 3 | bytes 24 | tf_op jit(solution)/shard_map/psum | solution.py:56
  123.8 0.6 fusion.9
  124.4 0.0 copy-start.4
  124.4 0.7 copy-done.4
  125.0 0.0 copy-start.3
  125.0 0.6 dynamic-slice.10
  125.6 0.1 copy-done.3
  125.7 0.6 dynamic-slice.6
  127.6 0.0 collective-permute-done.1
  127.6 0.2 concatenate.1
  127.8 0.7 constant_dynamic-slice_fusion
  128.4 0.0 collective-permute-done
  128.4 0.2 concatenate
  128.7 0.7 constant_dynamic-slice_fusion.1
  (7 shorter events, 0.1 us)
Async XLA Ops:
  2.0 0.7 copy-start.1
  10.3 0.8 copy-start
  10.3 0.8 copy-start.2
  54.1 73.5 %collective-permute-start.1 = (f32[12,768]{1,0:T(8,128)S(1)}, f32[12,768]{1,0:T(8,128)S(1)}, u32[]{:S(2)}, u32[]{:S(2)}) collective-permute-start(f32[12,768]{1,0:T(8,128)S(1)} %slice.13), channel_id=1, source_target_pairs={{0,8},{8,16},{16,24},{1,9},{9,17},{17,25},{2,10},{10,18},{18,26},{... | collective-permute-start | bytes 110600
  84.0 44.5 %collective-permute-start = (f32[28,768]{1,0:T(8,128)S(1)}, f32[28,768]{1,0:T(8,128)S(1)}, u32[]{:S(2)}, u32[]{:S(2)}) collective-permute-start(f32[28,768]{1,0:T(8,128)S(1)} %slice.12), channel_id=1, source_target_pairs={{0,1},{1,2},{2,3},{3,4},{4,5},{5,6},{6,7},{8,9},{9,10},{10,11},{11... | collective-permute-start | bytes 258056
  124.4 0.7 copy-start.4
  125.0 0.7 copy-start.3
where the time goes:
time: 130 us; the launch traced here: 129 us
  blocking collectives  113 us (87%)
  local copies, waits for them, and re-layouts  5.72 us (4%)
  between operations  3.36 us (3%)
  starting transfers between devices  3.04 us (2%)
  other arithmetic  2.98 us (2%)
  matrix products  1.67 us (1%)
    psum x1, blocking collectives, body(): totals = lax.psum(sums, ('blk', 'grp'))  38.1 us
    unnamed x2, blocking collectives  35.9 us
    all_gather x1, blocking collectives, body(): wide = lax.all_gather(wide_source, 'grp', axis=0, tiled=True)  31.7 us
    all_gather x1, blocking collectives, body(): narrow = lax.all_gather(narrow_source, 'blk', axis=0, tiled=True)  6.82 us
    unnamed x20, local copies, waits for them, and re-layouts  5.12 us
    unnamed x2, starting transfers between devices  3.04 us
  transfers between devices with their start and end apart: 2, of which 0 were waited for; matrix products, arithmetic and copies ran while one was open for 24% of the time, Pallas kernels for 0%

commit v1 on v0

v1 whole, which is shorter than its diff:
```python
import functools
import itertools

import jax
import jax.numpy as jnp
from jax import lax
from jax.experimental import pallas as pl
from jax.experimental.pallas import tpu as pltpu
from jax.sharding import PartitionSpec as P

MESH = pl.DeviceIdType.MESH


def layout(groups, members):
    cores = 2 if groups % 2 == 0 else 1
    sides = 2 if members % 2 == 0 else 1
    return cores, groups // cores, sides, members // sides


def kernel(
    groups,
    members,
    rows,
    pad,
    pic_ref,
    pic_mul_ref,
    cap_ref,
    cap_mul_ref,
    sharp_ref,
    shift_ref,
    loss_ref,
    image_grad_ref,
    text_grad_ref,
    temp_ref,
    bias_ref,
    stage,
    img,
    txt,
    img_part,
    txt_part,
    img_back,
    txt_back,
    near_out,
    near_in,
    far_out,
    far_in,
    img_send,
    img_recv,
    txt_send,
    txt_recv,
    img_back_send,
    img_back_recv,
    txt_back_send,
    txt_back_recv,
    near_send,
    near_recv,
    far_send,
    far_recv,
):
    cores, chips, sides, planes = layout(groups, members)
    b, g = lax.axis_index("blk"), lax.axis_index("grp")
    chip, core = b // cores, b % cores
    z, y = g // sides, g % sides
    offsets = list(itertools.product(range(sides), range(chips), range(cores)))
    n_img, n_txt = planes, len(offsets)

    def plane_peer(index, sign):
        dy, dx, dc = offsets[index]
        y2 = (y + (dy if sign > 0 else sides - dy)) % sides
        x2 = (chip + (dx if sign > 0 else chips - dx)) % chips
        c2 = (core + (dc if sign > 0 else cores - dc)) % cores
        return (x2 * cores + c2, z * sides + y2)

    def column_peer(index, sign):
        z2 = (z + (index if sign > 0 else planes - index)) % planes
        return (b, z2 * sides + y)

    barrier = pltpu.get_barrier_semaphore()
    for k in range(1, n_img):
        pl.semaphore_signal(barrier, inc=1, device_id=column_peer(k, 1), device_id_type=MESH)
    for k in range(1, n_txt):
        pl.semaphore_signal(barrier, inc=1, device_id=plane_peer(k, 1), device_id_type=MESH)

    def decode(codes_ref, mul_ref, slot):
        diagonal = lax.broadcasted_iota(jnp.int32, (rows, rows), 0) == lax.broadcasted_iota(
            jnp.int32, (rows, rows), 1
        )
        across = jnp.broadcast_to(mul_ref[...].reshape(1, rows), (rows, rows))
        scale = jnp.sum(jnp.where(diagonal, across, 0.0), axis=1, keepdims=True)
        stage[...] = jnp.zeros_like(stage)
        stage[0:rows, :] = scale * codes_ref[...].astype(jnp.float32)
        slot[0:pad, :] = stage[...].astype(jnp.bfloat16)

    def block(ref, k):
        return ref.at[pl.ds(k * pad, pad), :]

    decode(pic_ref, pic_mul_ref, img)
    decode(cap_ref, cap_mul_ref, txt)
    pl.semaphore_wait(barrier, n_img - 1 + n_txt - 1)

    copies = []

    def send(src, dst, send_sem, recv_sem, peer):
        copy = pltpu.make_async_remote_copy(
            src_ref=src,
            dst_ref=dst,
            send_sem=send_sem,
            recv_sem=recv_sem,
            device_id=peer,
            device_id_type=MESH,
        )
        copy.start()
        copies.append(copy)
        return copy

    gathers = []
    for k in range(max(n_img, n_txt) - 1, 0, -1):
        if k < n_txt:
            gathers.append(
                send(block(txt, 0), block(txt, k), txt_send.at[k], txt_recv.at[k], plane_peer(k, 1))
            )
        if k < n_img:
            gathers.append(
                send(block(img, 0), block(img, k), img_send.at[k], img_recv.at[k], column_peer(k, 1))
            )
    for copy in gathers:
        copy.wait_recv()

    sharp = sharp_ref[0]
    shift = shift_ref[0]
    images, texts = img[...], txt[...]
    dots = lax.dot_general(
        images, texts, (((1,), (1,)), ((), ())), preferred_element_type=jnp.float32
    )
    logits = sharp * dots + shift
    row = lax.broadcasted_iota(jnp.int32, dots.shape, 0)
    col = lax.broadcasted_iota(jnp.int32, dots.shape, 1)
    positive = (row == col) & (row < pad)
    real = (row % pad < rows) & (col % pad < rows)
    small = jnp.exp(-jnp.abs(logits))
    below = 1.0 / (1.0 + small)
    slopes = jnp.where(logits >= 0, below, small * below) - jnp.where(positive, 1.0, 0.0)
    terms = jnp.maximum(jnp.where(positive, -logits, logits), 0.0) + jnp.log1p(small)
    weights = (sharp * slopes).astype(jnp.bfloat16)

    def total(x):
        return jnp.sum(jnp.sum(x, axis=0, keepdims=True), axis=1, keepdims=True)

    lane = lax.broadcasted_iota(jnp.int32, near_out.shape, 0)
    near = jnp.where(
        lane == 0,
        total(jnp.where(real, terms, 0.0)),
        jnp.where(lane == 1, total(slopes * dots), total(jnp.where(real, slopes, 0.0))),
    )
    near_out[...] = near
    nears = [
        send(near_out, near_in.at[k], near_send.at[k], near_recv.at[k], plane_peer(k, 1))
        for k in range(1, n_txt)
    ]

    txt_total = lax.dot_general(
        weights, images, (((0,), (0,)), ((), ())), preferred_element_type=jnp.float32
    )
    txt_part[...] = txt_total.astype(jnp.bfloat16)
    txt_backs = [
        send(
            block(txt_part, k),
            txt_back.at[k],
            txt_back_send.at[k],
            txt_back_recv.at[k],
            plane_peer(k, -1),
        )
        for k in range(n_txt - 1, 0, -1)
    ]
    img_total = jnp.dot(weights, texts, preferred_element_type=jnp.float32)
    img_part[...] = img_total.astype(jnp.bfloat16)
    img_backs = [
        send(
            block(img_part, k),
            img_back.at[k],
            img_back_send.at[k],
            img_back_recv.at[k],
            column_peer(k, -1),
        )
        for k in range(n_img - 1, 0, -1)
    ]

    for k, copy in enumerate(nears, 1):
        copy.wait_recv()
        near = near + near_in[k]
    far_out[...] = near
    fars = [
        send(far_out, far_in.at[k], far_send.at[k], far_recv.at[k], column_peer(k, 1))
        for k in range(1, n_img)
    ]

    own = txt_total[0:pad]
    for k, copy in zip(range(n_txt - 1, 0, -1), txt_backs):
        copy.wait_recv()
        own = own + txt_back[k].astype(jnp.float32)
    text_grad_ref[...] = own[0:rows]
    own = img_total[0:pad]
    for k, copy in zip(range(n_img - 1, 0, -1), img_backs):
        copy.wait_recv()
        own = own + img_back[k].astype(jnp.float32)
    image_grad_ref[...] = own[0:rows]

    for k, copy in enumerate(fars, 1):
        copy.wait_recv()
        near = near + far_in[k]
    near = near / (rows * groups * members)
    loss_ref[0] = near[0, 0]
    temp_ref[0] = near[1, 0]
    bias_ref[0] = near[2, 0]
    for copy in copies:
        copy.wait_send()


def body(groups, members, pic, pic_mul, cap, cap_mul, sharp, shift):
    rows, width = pic.shape
    pad = -(-rows // 16) * 16
    cores, chips, sides, planes = layout(groups, members)
    n_img, n_txt = planes, sides * chips * cores
    vmem = pl.BlockSpec(memory_space=pltpu.VMEM)
    smem = pl.BlockSpec(memory_space=pltpu.SMEM)
    one = jax.ShapeDtypeStruct((1,), jnp.float32)
    grad = jax.ShapeDtypeStruct((rows, width), jnp.float32)
    bf16, f32, dma = jnp.bfloat16, jnp.float32, pltpu.SemaphoreType.DMA
    return pl.pallas_call(
        functools.partial(kernel, groups, members, rows, pad),
        out_shape=(one, grad, grad, one, one),
        in_specs=[vmem, vmem, vmem, vmem, smem, smem],
        out_specs=(smem, vmem, vmem, smem, smem),
        scratch_shapes=[
            pltpu.VMEM((pad, width), f32),
            pltpu.VMEM((n_img * pad, width), bf16),
            pltpu.VMEM((n_txt * pad, width), bf16),
            pltpu.VMEM((n_img * pad, width), bf16),
            pltpu.VMEM((n_txt * pad, width), bf16),
            pltpu.VMEM((n_img, pad, width), bf16),
            pltpu.VMEM((n_txt, pad, width), bf16),
            pltpu.VMEM((8, 128), f32),
            pltpu.VMEM((n_txt, 8, 128), f32),
            pltpu.VMEM((8, 128), f32),
            pltpu.VMEM((n_img, 8, 128), f32),
            dma((n_img,)),
            dma((n_img,)),
            dma((n_txt,)),
            dma((n_txt,)),
            dma((n_img,)),
            dma((n_img,)),
            dma((n_txt,)),
            dma((n_txt,)),
            dma((n_txt,)),
            dma((n_txt,)),
            dma((n_img,)),
            dma((n_img,)),
        ],
        compiler_params=pltpu.CompilerParams(
            collective_id=0, has_side_effects=True, vmem_limit_bytes=32 * 1024 * 1024
        ),
    )(pic, pic_mul, cap, cap_mul, sharp, shift)


def solution(mesh):
    placed = (
        P(("blk", "grp"), None),
        P(("blk", "grp")),
        P(("blk", "grp"), None),
        P(("blk", "grp")),
        P(),
        P(),
    )
    return jax.shard_map(
        functools.partial(body, mesh.shape["blk"], mesh.shape["grp"]),
        mesh=mesh,
        in_specs=placed,
        out_specs=(P(), P(("blk", "grp"), None), P(("blk", "grp"), None), P(), P()),
        check_vma=False,
    )
```

time: 130 us -> 30.8 us (0.24)
  blocking collectives: 113 us -> 0 us
  Pallas kernels: 0 us -> 20.4 us
  between operations: 3.36 us -> 7.24 us
  starting transfers between devices: 3.04 us -> 0 us
  other arithmetic: 2.98 us -> 0 us
  local copies, waits for them, and re-layouts: 5.72 us -> 2.88 us
  matrix products: 1.67 us -> 0 us
    all_gather x2 -> x0, blocking collectives: 38.6 us -> none  [the longest x1 31.7 us: body(): wide = lax.all_gather(wide_source, 'grp', axis=0, tiled=True)]
    psum x1 -> x0, blocking collectives: 38.1 us -> none  [body(): totals = lax.psum(sums, ('blk', 'grp'))]
    unnamed x2 -> x0, blocking collectives: 35.9 us -> none
    pallas_call x0 -> x1, Pallas kernels: none -> 20.4 us  [body(): pl.pallas_call(functools.partial(kernel, groups, members, rows, pad), out...]
    unnamed x2 -> x0, starting transfers between devices: 3.04 us -> none
    unnamed x20 -> x10, local copies, waits for them, and re-layouts: 5.12 us -> 2.88 us
    another operation x1 -> x0, other arithmetic: 2.02 us -> none  [score_block(): jnp.stack([jnp.sum(loss_terms), jnp.sum(slopes * dots), jnp.sum(slopes)])]
    dot_general x3 -> x0, matrix products: 1.67 us -> none  [the longest x1 1.06 us: score_block(): lax.dot_general(piece, wide, (((1,), (1,)), ((), ())), preferred_element_...]
  transfers between devices with their start and end apart: 2 -> 0, of which waited for: 0 -> 0; matrix products, arithmetic and copies ran while one was open for 24% -> 0% of each run, Pallas kernels for 0% -> 0%
where the time goes in v1:
time: 30.8 us; the launch traced here: 30.5 us
  Pallas kernels  20.4 us (66%)
  between operations  7.24 us (24%)
  local copies, waits for them, and re-layouts  2.88 us (9%)
    pallas_call x1, Pallas kernels, body(): pl.pallas_call(functools.partial(kernel, groups, members, rows, pad), out...  20.4 us
    unnamed x10, local copies, waits for them, and re-layouts  2.88 us

profile of v1, /device:TPU:0, one launch (start us, length us, event | category | flops | bytes accessed | tf_op | source)
XLA Modules:
  0.0 30.5 jit_solution(8507607712118152306)
XLA Ops:
  1.3 0.0 copy-start.2
  1.3 0.0 copy-start.3
  2.0 0.0 copy-done.2
  2.0 0.0 copy-done.3
  2.0 0.0 copy-start
  2.0 0.8 %copy-done = bf16[28,768]{1,0:T(8,128)(2,1)S(1)} copy-done((bf16[28,768]{1,0:T(8,128)(2,1)S(1)}, bf16[28,768]{1,0:T(8,128)(2,1)}, u32[]{:S(2)}) %copy-start) | copy-done | bytes 43032
  2.8 0.0 copy-start.1
  2.8 0.8 %copy-done.1 = bf16[28,768]{1,0:T(8,128)(2,1)S(1)} copy-done((bf16[28,768]{1,0:T(8,128)(2,1)S(1)}, bf16[28,768]{1,0:T(8,128)(2,1)}, u32[]{:S(2)}) %copy-start.1) | copy-done | bytes 43032
  3.6 20.4 %shard_map.101 = (f32[1]{0:T(128)}, f32[28,768]{1,0:T(8,128)S(1)}, f32[28,768]{1,0:T(8,128)S(1)}, f32[1]{0:T(128)}, f32[1]{0:T(128)}) custom-call(bf16[28,768]{1,0:T(8,128)(2,1)S(1)} %copy-done, f32[28]{0:T(128)S(1)} %copy-done.2, bf16[28,768]{1,0:T(8,128)(2,1)S(1)} %copy-done.1, f32[28]{0:T(128)S(1)} %copy-done.3, f32[1]{0:T(128)S(6)} %copy.16.sharp_ref, ...), custom_call_target="tpu_custom_call" | custom-call | tf_op jit(solution)/shard_map/pallas_call | solution.py:229
  24.6 0.6 %copy.19 = f32[28,768]{1,0:T(8,128)} copy(f32[28,768]{1,0:T(8,128)S(1)} %get-tuple-element.11) | data formatting | bytes 172032
  25.2 0.6 %copy.20 = f32[28,768]{1,0:T(8,128)} copy(f32[28,768]{1,0:T(8,128)S(1)} %get-tuple-element.12) | data formatting | bytes 172032
Async XLA Ops:
  1.3 0.7 %copy-start.2 = (f32[28]{0:T(128)S(1)}, f32[28]{0:T(128)}, u32[]{:S(2)}) copy-start(f32[28]{0:T(128)} %pic_mul_ref.1) | copy-start | bytes 340
  1.3 0.7 %copy-start.3 = (f32[28]{0:T(128)S(1)}, f32[28]{0:T(128)}, u32[]{:S(2)}) copy-start(f32[28]{0:T(128)} %cap_mul_ref.1) | copy-start | bytes 340
  2.0 0.8 %copy-start = (bf16[28,768]{1,0:T(8,128)(2,1)S(1)}, bf16[28,768]{1,0:T(8,128)(2,1)}, u32[]{:S(2)}) copy-start(bf16[28,768]{1,0:T(8,128)(2,1)} %pic_ref.1) | copy-start | bytes 129028
  2.8 0.8 %copy-start.1 = (bf16[28,768]{1,0:T(8,128)(2,1)S(1)}, bf16[28,768]{1,0:T(8,128)(2,1)}, u32[]{:S(2)}) copy-start(bf16[28,768]{1,0:T(8,128)(2,1)} %cap_ref.1) | copy-start | bytes 129028

commit v2 on v1

--- a/solution.py
+++ b/solution.py
@@ -22,17 +22,22 @@
     members,
     rows,
     pad,
+    pic_hbm,
+    pic_mul_hbm,
+    cap_hbm,
+    cap_mul_hbm,
+    sharp_hbm,
+    shift_hbm,
+    image_grad_ref,
+    text_grad_ref,
+    sums_ref,
     pic_ref,
     pic_mul_ref,
     cap_ref,
     cap_mul_ref,
     sharp_ref,
     shift_ref,
-    loss_ref,
-    image_grad_ref,
-    text_grad_ref,
-    temp_ref,
-    bias_ref,
+    load_sem,
     stage,
     img,
     txt,
@@ -75,6 +80,21 @@
         z2 = (z + (index if sign > 0 else planes - index)) % planes
         return (b, z2 * sides + y)
 
+    loads = [
+        pltpu.make_async_copy(src, dst, load_sem.at[i])
+        for i, (src, dst) in enumerate(
+            [
+                (pic_mul_hbm, pic_mul_ref),
+                (pic_hbm, pic_ref),
+                (cap_mul_hbm, cap_mul_ref),
+                (cap_hbm, cap_ref),
+                (sharp_hbm, sharp_ref),
+                (shift_hbm, shift_ref),
+            ]
+        )
+    ]
+    for load in loads:
+        load.start()
     barrier = pltpu.get_barrier_semaphore()
     for k in range(1, n_img):
         pl.semaphore_signal(barrier, inc=1, device_id=column_peer(k, 1), device_id_type=MESH)
@@ -94,8 +114,9 @@
     def block(ref, k):
         return ref.at[pl.ds(k * pad, pad), :]
 
+    loads[0].wait()
+    loads[1].wait()
     decode(pic_ref, pic_mul_ref, img)
-    decode(cap_ref, cap_mul_ref, txt)
     pl.semaphore_wait(barrier, n_img - 1 + n_txt - 1)
 
     copies = []
@@ -113,16 +134,19 @@
         copies.append(copy)
         return copy
 
-    gathers = []
-    for k in range(max(n_img, n_txt) - 1, 0, -1):
-        if k < n_txt:
-            gathers.append(
-                send(block(txt, 0), block(txt, k), txt_send.at[k], txt_recv.at[k], plane_peer(k, 1))
-            )
-        if k < n_img:
-            gathers.append(
-                send(block(img, 0), block(img, k), img_send.at[k], img_recv.at[k], column_peer(k, 1))
-            )
+    gathers = [
+        send(block(img, 0), block(img, k), img_send.at[k], img_recv.at[k], column_peer(k, 1))
+        for k in range(n_img - 1, 0, -1)
+    ]
+    loads[2].wait()
+    loads[3].wait()
+    decode(cap_ref, cap_mul_ref, txt)
+    gathers += [
+        send(block(txt, 0), block(txt, k), txt_send.at[k], txt_recv.at[k], plane_peer(k, 1))
+        for k in range(n_txt - 1, 0, -1)
+    ]
+    loads[4].wait()
+    loads[5].wait()
     for copy in gathers:
         copy.wait_recv()
 
@@ -208,12 +232,24 @@
     for k, copy in enumerate(fars, 1):
         copy.wait_recv()
         near = near + far_in[k]
-    near = near / (rows * groups * members)
-    loss_ref[0] = near[0, 0]
-    temp_ref[0] = near[1, 0]
-    bias_ref[0] = near[2, 0]
+    sums_ref[...] = near / (rows * groups * members)
     for copy in copies:
         copy.wait_send()
+
+
+def deliver(image_ref, text_ref, sums_ref, loss_ref, image_out, text_out, temp_ref, bias_ref, sem):
+    copies = [
+        pltpu.make_async_copy(src, dst, sem.at[i])
+        for i, (src, dst) in enumerate([(image_ref, image_out), (text_ref, text_out)])
+    ]
+    for copy in copies:
+        copy.start()
+    sums = sums_ref[...]
+    loss_ref[0] = sums[0, 0]
+    temp_ref[0] = sums[1, 0]
+    bias_ref[0] = sums[2, 0]
+    for copy in copies:
+        copy.wait()
 
 
 def body(groups, members, pic, pic_mul, cap, cap_mul, sharp, shift):
@@ -223,15 +259,24 @@
     n_img, n_txt = planes, sides * chips * cores
     vmem = pl.BlockSpec(memory_space=pltpu.VMEM)
     smem = pl.BlockSpec(memory_space=pltpu.SMEM)
-    one = jax.ShapeDtypeStruct((1,), jnp.float32)
-    grad = jax.ShapeDtypeStruct((rows, width), jnp.float32)
+    hbm = pl.BlockSpec(memory_space=pltpu.HBM)
     bf16, f32, dma = jnp.bfloat16, jnp.float32, pltpu.SemaphoreType.DMA
-    return pl.pallas_call(
+    one = jax.ShapeDtypeStruct((1,), f32)
+    grad = jax.ShapeDtypeStruct((rows, width), f32)
+    tile = jax.ShapeDtypeStruct((8, 128), f32)
+    image_grad, text_grad, sums = pl.pallas_call(
         functools.partial(kernel, groups, members, rows, pad),
-        out_shape=(one, grad, grad, one, one),
-        in_specs=[vmem, vmem, vmem, vmem, smem, smem],
-        out_specs=(smem, vmem, vmem, smem, smem),
+        out_shape=(grad, grad, tile),
+        in_specs=[hbm] * 6,
+        out_specs=(vmem, vmem, vmem),
         scratch_shapes=[
+            pltpu.VMEM((rows, width), bf16),
+            pltpu.VMEM((rows,), f32),
+            pltpu.VMEM((rows, width), bf16),
+            pltpu.VMEM((rows,), f32),
+            pltpu.SMEM((1,), f32),
+            pltpu.SMEM((1,), f32),
+            dma((6,)),
             pltpu.VMEM((pad, width), f32),
             pltpu.VMEM((n_img * pad, width), bf16),
             pltpu.VMEM((n_txt * pad, width), bf16),
@@ -257,9 +302,16 @@
             dma((n_img,)),
         ],
         compiler_params=pltpu.CompilerParams(
-            collective_id=0, has_side_effects=True, vmem_limit_bytes=32 * 1024 * 1024
+            collective_id=0, has_side_effects=True, vmem_limit_bytes=64 * 1024 * 1024
         ),
     )(pic, pic_mul, cap, cap_mul, sharp, shift)
+    return pl.pallas_call(
+        deliver,
+        out_shape=(one, grad, grad, one, one),
+        in_specs=[vmem] * 3,
+        out_specs=(smem, hbm, hbm, smem, smem),
+        scratch_shapes=[dma((2,))],
+    )(image_grad, text_grad, sums)
 
 
 def solution(mesh):

time: 30.8 us -> 25.1 us (0.81)
  between operations: 7.24 us -> 1.93 us
  local copies, waits for them, and re-layouts: 2.88 us -> 0 us
  Pallas kernels: 20.4 us -> 22.9 us
    unnamed x10 -> x0, local copies, waits for them, and re-layouts: 2.88 us -> none
    pallas_call x0 -> x1, Pallas kernels: none -> 2.17 us  [body(): pl.pallas_call(deliver, out_shape=(one, grad, grad, one, one), in_specs=[...]
    pallas_call x1, Pallas kernels: 20.4 us -> 20.7 us  [body(): pl.pallas_call(functools.partial(kernel, groups, members, rows, pad), out...]
where the time goes in v2:
time: 25.1 us; the launch traced here: 24.8 us
  Pallas kernels  22.9 us (91%)
  between operations  1.93 us (8%)
    pallas_call x1, Pallas kernels, body(): pl.pallas_call(functools.partial(kernel, groups, members, rows, pad), out...  20.7 us
    pallas_call x1, Pallas kernels, body(): pl.pallas_call(deliver, out_shape=(one, grad, grad, one, one), in_specs=[...  2.17 us

profile of v2, /device:TPU:0, one launch (start us, length us, event | category | flops | bytes accessed | tf_op | source)
XLA Modules:
  0.0 24.8 jit_solution(15097882233213450161)
XLA Ops:
  1.9 20.7 %shard_map.101 = (f32[28,768]{1,0:T(8,128)}, f32[28,768]{1,0:T(8,128)}, f32[8,128]{1,0:T(8,128)}) custom-call(bf16[28,768]{1,0:T(8,128)(2,1)} %pic_hbm.1, f32[28]{0:T(128)} %pic_mul_hbm.1, bf16[28,768]{1,0:T(8,128)(2,1)} %cap_hbm.1, f32[28]{0:T(128)} %cap_mul_hbm.1, f32[1]{0:T(128)S(6)} %copy.11.sharp_hbm, f32[1]{0:T(128)S(6)} %copy.12.shift_hbm), custom_call_target="tpu_custom_call" | custom-call | tf_op jit(solution)/shard_map/pallas_call | solution.py:267
  22.7 2.2 %shard_map.102 = (f32[1]{0:T(128)}, f32[28,768]{1,0:T(8,128)}, f32[28,768]{1,0:T(8,128)}, f32[1]{0:T(128)}, f32[1]{0:T(128)}) custom-call(f32[28,768]{1,0:T(8,128)} %get-tuple-element.8.image_ref, f32[28,768]{1,0:T(8,128)} %get-tuple-element.9.text_ref, f32[8,128]{1,0:T(8,128)} %get-tuple-element.10.sums_ref), custom_call_target="tpu_custom_call" | custom-call | tf_op jit(solution)/shard_map/pallas_call | solution.py:308

commit v3 on v2

--- a/solution.py
+++ b/solution.py
@@ -266,7 +266,7 @@
     tile = jax.ShapeDtypeStruct((8, 128), f32)
     image_grad, text_grad, sums = pl.pallas_call(
         functools.partial(kernel, groups, members, rows, pad),
-        out_shape=(grad, grad, tile),
+        out_shape=(pltpu.VMEM((rows, width), f32), pltpu.VMEM((rows, width), f32), pltpu.VMEM((8, 128), f32)),
         in_specs=[hbm] * 6,
         out_specs=(vmem, vmem, vmem),
         scratch_shapes=[
@@ -302,7 +302,7 @@
             dma((n_img,)),
         ],
         compiler_params=pltpu.CompilerParams(
-            collective_id=0, has_side_effects=True, vmem_limit_bytes=64 * 1024 * 1024
+            collective_id=0, has_side_effects=True, vmem_limit_bytes=63 * 1024 * 1024
         ),
     )(pic, pic_mul, cap, cap_mul, sharp, shift)
     return pl.pallas_call(
@@ -311,6 +311,7 @@
         in_specs=[vmem] * 3,
         out_specs=(smem, hbm, hbm, smem, smem),
         scratch_shapes=[dma((2,))],
+        compiler_params=pltpu.CompilerParams(vmem_limit_bytes=4 * 1024 * 1024),
     )(image_grad, text_grad, sums)
 
 

time: 25.1 us -> 23.4 us (0.932)
  Pallas kernels: 22.9 us -> 21.3 us
    pallas_call x1, Pallas kernels: 2.17 us -> 1.23 us  [body(): pl.pallas_call(deliver, out_shape=(one, grad, grad, one, one), in_specs=[...]
    pallas_call x1, Pallas kernels: 20.7 us -> 20.1 us  [body(): pl.pallas_call(functools.partial(kernel, groups, members, rows, pad), out...]
where the time goes in v3:
time: 23.4 us; the launch traced here: 23.2 us
  Pallas kernels  21.3 us (91%)
  between operations  1.93 us (8%)
    pallas_call x1, Pallas kernels, body(): pl.pallas_call(functools.partial(kernel, groups, members, rows, pad), out...  20.1 us
    pallas_call x1, Pallas kernels, body(): pl.pallas_call(deliver, out_shape=(one, grad, grad, one, one), in_specs=[...  1.23 us

profile of v3, /device:TPU:0, one launch (start us, length us, event | category | flops | bytes accessed | tf_op | source)
XLA Modules:
  0.0 23.2 jit_solution(1285977930052523717)
XLA Ops:
  1.9 20.1 %shard_map.101 = (f32[28,768]{1,0:T(8,128)S(1)}, f32[28,768]{1,0:T(8,128)S(1)}, f32[8,128]{1,0:T(8,128)S(1)}) custom-call(bf16[28,768]{1,0:T(8,128)(2,1)} %pic_hbm.1, f32[28]{0:T(128)} %pic_mul_hbm.1, bf16[28,768]{1,0:T(8,128)(2,1)} %cap_hbm.1, f32[28]{0:T(128)} %cap_mul_hbm.1, f32[1]{0:T(128)S(6)} %copy.11.sharp_hbm, f32[1]{0:T(128)S(6)} %copy.12.shift_hbm), custom_call_target="tpu_custom_call" | custom-call | tf_op jit(solution)/shard_map/pallas_call | solution.py:267
  22.0 1.2 %shard_map.102 = (f32[1]{0:T(128)}, f32[28,768]{1,0:T(8,128)}, f32[28,768]{1,0:T(8,128)}, f32[1]{0:T(128)}, f32[1]{0:T(128)}) custom-call(f32[28,768]{1,0:T(8,128)S(1)} %get-tuple-element.8.image_ref, f32[28,768]{1,0:T(8,128)S(1)} %get-tuple-element.9.text_ref, f32[8,128]{1,0:T(8,128)S(1)} %get-tuple-element.10.sums_ref), custom_call_target="tpu_custom_call" | custom-call | tf_op jit(solution)/shard_map/pallas_call | solution.py:308

commit v4 on v3

--- a/solution.py
+++ b/solution.py
@@ -80,6 +80,12 @@
         z2 = (z + (index if sign > 0 else planes - index)) % planes
         return (b, z2 * sides + y)
 
+    barrier = pltpu.get_barrier_semaphore()
+    for k in range(n_img - 1, 0, -1):
+        pl.semaphore_signal(barrier, inc=1, device_id=column_peer(k, 1), device_id_type=MESH)
+    for k in range(n_txt - 1, 0, -1):
+        pl.semaphore_signal(barrier, inc=1, device_id=plane_peer(k, 1), device_id_type=MESH)
+
     loads = [
         pltpu.make_async_copy(src, dst, load_sem.at[i])
         for i, (src, dst) in enumerate(
@@ -95,25 +101,19 @@
     ]
     for load in loads:
         load.start()
-    barrier = pltpu.get_barrier_semaphore()
-    for k in range(1, n_img):
-        pl.semaphore_signal(barrier, inc=1, device_id=column_peer(k, 1), device_id_type=MESH)
-    for k in range(1, n_txt):
-        pl.semaphore_signal(barrier, inc=1, device_id=plane_peer(k, 1), device_id_type=MESH)
-
     def decode(codes_ref, mul_ref, slot):
         diagonal = lax.broadcasted_iota(jnp.int32, (rows, rows), 0) == lax.broadcasted_iota(
             jnp.int32, (rows, rows), 1
         )
         across = jnp.broadcast_to(mul_ref[...].reshape(1, rows), (rows, rows))
         scale = jnp.sum(jnp.where(diagonal, across, 0.0), axis=1, keepdims=True)
-        stage[...] = jnp.zeros_like(stage)
         stage[0:rows, :] = scale * codes_ref[...].astype(jnp.float32)
         slot[0:pad, :] = stage[...].astype(jnp.bfloat16)
 
     def block(ref, k):
         return ref.at[pl.ds(k * pad, pad), :]
 
+    stage[...] = jnp.zeros_like(stage)
     loads[0].wait()
     loads[1].wait()
     decode(pic_ref, pic_mul_ref, img)
@@ -182,20 +182,23 @@
         for k in range(1, n_txt)
     ]
 
-    txt_total = lax.dot_general(
-        weights, images, (((0,), (0,)), ((), ())), preferred_element_type=jnp.float32
-    )
-    txt_part[...] = txt_total.astype(jnp.bfloat16)
-    txt_backs = [
-        send(
-            block(txt_part, k),
-            txt_back.at[k],
-            txt_back_send.at[k],
-            txt_back_recv.at[k],
-            plane_peer(k, -1),
-        )
-        for k in range(n_txt - 1, 0, -1)
-    ]
+    txt_backs = []
+    half = (n_txt // 2) * pad
+    for low, high in ((half, n_txt * pad), (0, half)):
+        txt_total = lax.dot_general(
+            weights[:, low:high], images, (((0,), (0,)), ((), ())), preferred_element_type=jnp.float32
+        )
+        txt_part[low:high, :] = txt_total.astype(jnp.bfloat16)
+        for k in range(high // pad - 1, max(low // pad, 1) - 1, -1):
+            txt_backs.append(
+                send(
+                    block(txt_part, k),
+                    txt_back.at[k],
+                    txt_back_send.at[k],
+                    txt_back_recv.at[k],
+                    plane_peer(k, -1),
+                )
+            )
     img_total = jnp.dot(weights, texts, preferred_element_type=jnp.float32)
     img_part[...] = img_total.astype(jnp.bfloat16)
     img_backs = [
@@ -237,17 +240,18 @@
         copy.wait_send()
 
 
-def deliver(image_ref, text_ref, sums_ref, loss_ref, image_out, text_out, temp_ref, bias_ref, sem):
-    copies = [
-        pltpu.make_async_copy(src, dst, sem.at[i])
-        for i, (src, dst) in enumerate([(image_ref, image_out), (text_ref, text_out)])
-    ]
-    for copy in copies:
-        copy.start()
+def deliver(
+    image_ref, text_ref, sums_ref, loss_out, image_out, text_out, temp_out, bias_out, held, sem
+):
+    pairs = [(image_ref, image_out), (text_ref, text_out)]
+    pairs += [(held.at[i], out) for i, out in enumerate((loss_out, temp_out, bias_out))]
+    copies = [pltpu.make_async_copy(src, dst, sem.at[i]) for i, (src, dst) in enumerate(pairs)]
+    copies[0].start()
+    copies[1].start()
     sums = sums_ref[...]
-    loss_ref[0] = sums[0, 0]
-    temp_ref[0] = sums[1, 0]
-    bias_ref[0] = sums[2, 0]
+    for i in range(3):
+        held[i, 0] = sums[i, 0]
+        copies[2 + i].start()
     for copy in copies:
         copy.wait()
 
@@ -258,7 +262,6 @@
     cores, chips, sides, planes = layout(groups, members)
     n_img, n_txt = planes, sides * chips * cores
     vmem = pl.BlockSpec(memory_space=pltpu.VMEM)
-    smem = pl.BlockSpec(memory_space=pltpu.SMEM)
     hbm = pl.BlockSpec(memory_space=pltpu.HBM)
     bf16, f32, dma = jnp.bfloat16, jnp.float32, pltpu.SemaphoreType.DMA
     one = jax.ShapeDtypeStruct((1,), f32)
@@ -309,8 +312,8 @@
         deliver,
         out_shape=(one, grad, grad, one, one),
         in_specs=[vmem] * 3,
-        out_specs=(smem, hbm, hbm, smem, smem),
-        scratch_shapes=[dma((2,))],
+        out_specs=(hbm, hbm, hbm, hbm, hbm),
+        scratch_shapes=[pltpu.SMEM((3, 1), f32), dma((5,))],
         compiler_params=pltpu.CompilerParams(vmem_limit_bytes=4 * 1024 * 1024),
     )(image_grad, text_grad, sums)
 

time: 23.4 us -> 22.6 us (0.966)
  Pallas kernels: 21.3 us -> 20.5 us
    pallas_call x1, Pallas kernels: 1.23 us -> 0.75 us  [body(): pl.pallas_call(deliver, out_shape=(one, grad, grad, one, one), in_specs=[...]
    pallas_call x1, Pallas kernels: 20.1 us -> 19.8 us  [body(): pl.pallas_call(functools.partial(kernel, groups, members, rows, pad), out...]
where the time goes in v4:
time: 22.6 us; the launch traced here: 22.5 us
  Pallas kernels  20.5 us (91%)
  between operations  1.93 us (9%)
    pallas_call x1, Pallas kernels, body(): pl.pallas_call(functools.partial(kernel, groups, members, rows, pad), out...  19.8 us
    pallas_call x1, Pallas kernels, body(): pl.pallas_call(deliver, out_shape=(one, grad, grad, one, one), in_specs=[...  0.75 us

profile of v4, /device:TPU:0, one launch (start us, length us, event | category | flops | bytes accessed | tf_op | source)
XLA Modules:
  0.0 22.5 jit_solution(5779214463896472123)
XLA Ops:
  1.9 19.8 %shard_map.101 = (f32[28,768]{1,0:T(8,128)S(1)}, f32[28,768]{1,0:T(8,128)S(1)}, f32[8,128]{1,0:T(8,128)S(1)}) custom-call(bf16[28,768]{1,0:T(8,128)(2,1)} %pic_hbm.1, f32[28]{0:T(128)} %pic_mul_hbm.1, bf16[28,768]{1,0:T(8,128)(2,1)} %cap_hbm.1, f32[28]{0:T(128)} %cap_mul_hbm.1, f32[1]{0:T(128)S(6)} %copy.11.sharp_hbm, f32[1]{0:T(128)S(6)} %copy.12.shift_hbm), custom_call_target="tpu_custom_call" | custom-call | tf_op jit(solution)/shard_map/pallas_call | solution.py:270
  21.7 0.7 %shard_map.102 = (f32[1]{0:T(128)}, f32[28,768]{1,0:T(8,128)}, f32[28,768]{1,0:T(8,128)}, f32[1]{0:T(128)}, f32[1]{0:T(128)}) custom-call(f32[28,768]{1,0:T(8,128)S(1)} %get-tuple-element.8.image_ref, f32[28,768]{1,0:T(8,128)S(1)} %get-tuple-element.9.text_ref, f32[8,128]{1,0:T(8,128)S(1)} %get-tuple-element.10.sums_ref), custom_call_target="tpu_custom_call" | custom-call | tf_op jit(solution)/shard_map/pallas_call | solution.py:311

commit v5 on v4

--- a/solution.py
+++ b/solution.py
@@ -141,12 +141,27 @@
     loads[2].wait()
     loads[3].wait()
     decode(cap_ref, cap_mul_ref, txt)
-    gathers += [
-        send(block(txt, 0), block(txt, k), txt_send.at[k], txt_recv.at[k], plane_peer(k, 1))
-        for k in range(n_txt - 1, 0, -1)
-    ]
+    direct = [k for k in range(n_txt - 1, 0, -1) if k % cores == 0] + list(range(cores - 1, 0, -1))
+    arrivals = {}
+    for k in direct:
+        arrivals[k] = send(
+            block(txt, 0), block(txt, k), txt_send.at[k], txt_recv.at[k], plane_peer(k, 1)
+        )
     loads[4].wait()
     loads[5].wait()
+    for k in sorted(arrivals, key=lambda k: offsets[k][0] + (offsets[k][1] > 0)):
+        arrivals[k].wait_recv()
+        if k >= cores:
+            for c in range(1, cores):
+                gathers.append(
+                    send(
+                        block(txt, k),
+                        block(txt, k + c),
+                        txt_send.at[k + c],
+                        txt_recv.at[k + c],
+                        plane_peer(c, 1),
+                    )
+                )
     for copy in gathers:
         copy.wait_recv()
 

time: 22.6 us -> 22.1 us (0.978)
  Pallas kernels: 20.5 us -> 20 us
    pallas_call x1, Pallas kernels: 19.8 us -> 19.3 us  [body(): pl.pallas_call(functools.partial(kernel, groups, members, rows, pad), out...]
where the time goes in v5:
time: 22.1 us; the launch traced here: 22 us
  Pallas kernels  20 us (90%)
  between operations  1.93 us (9%)
    pallas_call x1, Pallas kernels, body(): pl.pallas_call(functools.partial(kernel, groups, members, rows, pad), out...  19.3 us
    pallas_call x1, Pallas kernels, body(): pl.pallas_call(deliver, out_shape=(one, grad, grad, one, one), in_specs=[...  0.75 us

profile of v5, /device:TPU:0, one launch (start us, length us, event | category | flops | bytes accessed | tf_op | source)
XLA Modules:
  0.0 22.0 jit_solution(1010697173778842609)
XLA Ops:
  1.9 19.3 %shard_map.101 = (f32[28,768]{1,0:T(8,128)S(1)}, f32[28,768]{1,0:T(8,128)S(1)}, f32[8,128]{1,0:T(8,128)S(1)}) custom-call(bf16[28,768]{1,0:T(8,128)(2,1)} %pic_hbm.1, f32[28]{0:T(128)} %pic_mul_hbm.1, bf16[28,768]{1,0:T(8,128)(2,1)} %cap_hbm.1, f32[28]{0:T(128)} %cap_mul_hbm.1, f32[1]{0:T(128)S(6)} %copy.11.sharp_hbm, f32[1]{0:T(128)S(6)} %copy.12.shift_hbm), custom_call_target="tpu_custom_call" | custom-call | tf_op jit(solution)/shard_map/pallas_call | solution.py:285
  21.2 0.7 %shard_map.102 = (f32[1]{0:T(128)}, f32[28,768]{1,0:T(8,128)}, f32[28,768]{1,0:T(8,128)}, f32[1]{0:T(128)}, f32[1]{0:T(128)}) custom-call(f32[28,768]{1,0:T(8,128)S(1)} %get-tuple-element.8.image_ref, f32[28,768]{1,0:T(8,128)S(1)} %get-tuple-element.9.text_ref, f32[8,128]{1,0:T(8,128)S(1)} %get-tuple-element.10.sums_ref), custom_call_target="tpu_custom_call" | custom-call | tf_op jit(solution)/shard_map/pallas_call | solution.py:326
